TPU v7x, 512 devices: a whole 4x4x16 slice. The times are simulated.
512 devices in a mesh: ctx: 128 (over z, x, core), ch: 4 (over y).
Axes of the slice: x: 4, y: 4, z: 16, core: 2. Of those that a mesh axis runs over, the one named last changes fastest.
Arguments:
- projected: bfloat16 [3, 16384, 4096], P(None, 'ctx', 'ch'), may hold values from -6 to 6
- short_filter: float32 [3, 3, 4096], P(None, None, 'ch'), may hold values from -3.5 to 3.5
- residues: float32 [4096, 16], P('ch'), may hold values from -5 to 5
- decays: float32 [4096, 16], P('ch'), as said below
- skip: float32 [4096], P('ch'), may hold values from -1 to 1
- out_weight: bfloat16 [4096, 4096], P('ch', 'ctx'), may hold values from -0.09375 to 0.09375
Outputs:
- result: bfloat16 [16384, 4096], P('ctx', 'ch')
Inputs may be any that keep to these rules, and one draw needn't show every extreme that they name: `decays`: decay rates of the modal poles, at least 0.5 / 16384 and at most 1 / 32.
All inputs are finite; a program needn't handle non-finite values.
Results may differ from a plain program's by a relative error of at most 0.02.
Values may be sent and summed in bfloat16 or wider, within the bound.
A program may use at most 128 MiB of HBM per device.

v0:
```python
import math

import jax
import jax.numpy as jnp
from jax import lax
from jax.sharding import PartitionSpec as P


def passed_along(value, axis, steps):
    count = lax.axis_size(axis)
    initial, last = (max(0, -steps), min(count, count - steps))
    return lax.ppermute(value, axis, [(source, source + steps) for source in range(initial, last)])


def product(form, left, right):
    return jnp.einsum(form, left, right, precision=lax.Precision.HIGHEST)


def angles(first, second, period):
    turns = first[:, None] * second[None, :] % period
    return 2.0 * math.pi / period * turns.astype(jnp.float32)


def rotate(real_part, imag_part, phase):
    cosine = jnp.cos(phase)[:, :, None]
    sine = jnp.sin(phase)[:, :, None]
    return (real_part * cosine + imag_part * sine, imag_part * cosine - real_part * sine)


def on_device(projected, short_filter, residues, decays, skip, out_weight):
    devices = lax.axis_size("ctx")
    place = lax.axis_index("ctx")
    rows_dev = projected.shape[1]
    width = projected.shape[2]
    share = rows_dev // devices
    period = 2 * devices * rows_dev
    taps = short_filter.shape[1]
    rims = passed_along(projected[:, rows_dev - (taps - 1) :, :], "ctx", 1)
    extended = jnp.concatenate([rims, projected], axis=1).astype(jnp.float32)
    shorts = jnp.zeros(projected.shape, jnp.float32)
    for offset in range(taps):
        begin = taps - 1 - offset
        shorts = (
            shorts + short_filter[:, offset, None, :] * extended[:, begin : begin + rows_dev, :]
        )
    mixed_in = (shorts[1] * shorts[2]).astype(jnp.bfloat16)
    rates = decays.T
    amplitudes = (residues * jnp.sqrt(decays)).T
    fine = jnp.arange(rows_dev, dtype=jnp.int32)
    blocks = lax.all_to_all(mixed_in[None], "ctx", split_axis=1, concat_axis=0, tiled=True)
    block_ids = jnp.arange(devices, dtype=jnp.int32)
    coarse = jnp.arange(2 * devices, dtype=jnp.int32)
    coarse_phase = angles(coarse, block_ids, 2 * devices)
    coarse_cos = jnp.cos(coarse_phase)
    coarse_sin = jnp.sin(coarse_phase)
    local_rows = place * share + jnp.arange(share, dtype=jnp.int32)
    spread_phase = angles(coarse, local_rows, period)
    fine_phase = angles(fine, fine, rows_dev)
    fine_cos = jnp.cos(fine_phase)
    fine_sin = jnp.sin(fine_phase)

    def first_section(values):
        real_part = product("ka,arc->krc", coarse_cos, values)
        imag_part = -product("ka,arc->krc", coarse_sin, values)
        return rotate(real_part, imag_part, spread_phase)

    def last_section(real_part, imag_part):
        new_real = product("kb,jbc->jkc", fine_cos, real_part) + product(
            "kb,jbc->jkc", fine_sin, imag_part
        )
        new_imag = product("kb,jbc->jkc", fine_cos, imag_part) - product(
            "kb,jbc->jkc", fine_sin, real_part
        )
        return (new_real, new_imag)

    first_real, first_imag = first_section(blocks.astype(jnp.float32))
    positions = (block_ids[:, None] * rows_dev + local_rows[None, :]).astype(jnp.float32)

    def add_mode(mode, total):
        rate = lax.dynamic_index_in_dim(rates, mode, 0, False)
        amplitude = lax.dynamic_index_in_dim(amplitudes, mode, 0, False)
        return total + amplitude * jnp.exp(-rate * positions[:, :, None])

    filter_taps = lax.fori_loop(
        0, rates.shape[0], add_mode, jnp.zeros((devices, share, width), jnp.float32)
    )
    filter_real, filter_imag = first_section(filter_taps)
    signal_real, signal_imag, kernel_real, kernel_imag = (
        lax.all_to_all(
            first_real.astype(jnp.bfloat16), "ctx", split_axis=0, concat_axis=1, tiled=True
        ).astype(first_real.dtype),
        lax.all_to_all(
            first_imag.astype(jnp.bfloat16), "ctx", split_axis=0, concat_axis=1, tiled=True
        ).astype(first_imag.dtype),
        lax.all_to_all(
            filter_real.astype(jnp.bfloat16), "ctx", split_axis=0, concat_axis=1, tiled=True
        ).astype(filter_real.dtype),
        lax.all_to_all(
            filter_imag.astype(jnp.bfloat16), "ctx", split_axis=0, concat_axis=1, tiled=True
        ).astype(filter_imag.dtype),
    )
    kernel_real, kernel_imag = last_section(kernel_real, kernel_imag)
    signal_real, signal_imag = last_section(signal_real, signal_imag)
    joint_real = signal_real * kernel_real - signal_imag * kernel_imag
    joint_imag = signal_real * kernel_imag + signal_imag * kernel_real
    back_real = product("bk,jkc->jbc", fine_cos, joint_real) - product(
        "bk,jkc->jbc", fine_sin, joint_imag
    )
    back_imag = product("bk,jkc->jbc", fine_cos, joint_imag) + product(
        "bk,jkc->jbc", fine_sin, joint_real
    )
    back_real, back_imag = (
        lax.all_to_all(
            back_real.astype(jnp.bfloat16), "ctx", split_axis=1, concat_axis=0, tiled=True
        ).astype(back_real.dtype),
        lax.all_to_all(
            back_imag.astype(jnp.bfloat16), "ctx", split_axis=1, concat_axis=0, tiled=True
        ).astype(back_imag.dtype),
    )
    back_real, back_imag = rotate(back_real, back_imag, -spread_phase)
    rebuilt = (
        product("ka,krc->arc", coarse_cos, back_real)
        - product("ka,krc->arc", coarse_sin, back_imag)
    ) / period
    convolved = lax.all_to_all(
        rebuilt.astype(jnp.bfloat16), "ctx", split_axis=0, concat_axis=1, tiled=True
    ).astype(rebuilt.dtype)[0]
    gated = (shorts[0] * (convolved + skip * mixed_in.astype(jnp.float32))).astype(jnp.bfloat16)
    partial_sum = jnp.dot(
        gated,
        lax.all_gather(out_weight, "ctx", axis=1, tiled=True),
        preferred_element_type=jnp.float32,
    )
    total = lax.psum(partial_sum.astype(jnp.bfloat16), "ch").astype(jnp.float32)
    columns = partial_sum.shape[1] // lax.axis_size("ch")
    total = lax.dynamic_slice_in_dim(total, lax.axis_index("ch") * columns, columns, 1)
    return total.astype(jnp.bfloat16)


def solution(mesh):
    return jax.shard_map(
        on_device,
        mesh=mesh,
        in_specs=(
            P(None, "ctx", "ch"),
            P(None, None, "ch"),
            P("ch", None),
            P("ch", None),
            P("ch"),
            P("ch", "ctx"),
        ),
        out_specs=P("ctx", "ch"),
        check_vma=False,
    )
```

profile of v0, /device:TPU:1, one launch (start us, length us, event | category | flops | bytes accessed | tf_op | source)
XLA Modules:
  0.0 459.9 jit_solution(13193010133720526219)
XLA Ops:
  7.4 4.5 collective-permute-start
  13.8 2.4 collective-permute-done
  16.2 1.4 maximum_convert_fusion
  19.3 1.4 fusion.186
  21.3 2.1 reduce.4
  24.2 17.7 %all-to-all-start = ((bf16[128,2,512]{2,1,0:T(2,128)(2,1)}), bf16[128,2,512]{2,1,0:T(2,128)(2,1)S(1)}, u32[]{:S(2)}, u32[]{:S(2)}) async-start(bf16[128,2,512]{2,1,0:T(2,128)(2,1)} %reshape.297), calls=%async_computation | async-start | bytes 524288 | tf_op jit(solution)/shard_map/all_to_all | solution.py:50
  42.0 30.3 %while.14 = (s32[]{:T(128)}, f32[128,1,1024]{2,1,0:T(1,128)S(1)}, f32[16,1024]{1,0:T(8,128)S(1)}, f32[16,1024]{1,0:T(8,128)}, s32[]{:T(128)}, /*index=5*/s32[]{:T(128)}, s32[]{:T(128)}) while((s32[]{:T(128)}, f32[128,1,1024]{2,1,0:T(1,128)S(1)}, f32[16,1024]{1,0:T(8,128)S(1)}, f32[16,1024]{1,0:T(8,128)}, s32[]{:T(128)}, ...), condition=%wide.region_1.2_spmd.clone, body=%wide.region_0.1_spmd.clone.sunk | while | flops 525699 | bytes 1074271 | solution.py:84
  72.4 1.5 convolution_negate_fusion.1
  73.9 1.5 fusion.33
  76.7 2.5 fusion.28
  79.1 2.0 reduce.6
  82.1 16.1 %all-to-all-start.3 = ((bf16[128,2,1024]{2,1,0:T(2,128)(2,1)}), bf16[128,2,1024]{2,1,0:T(2,128)(2,1)S(1)}, u32[]{:S(2)}, u32[]{:S(2)}) async-start(bf16[128,2,1024]{2,1,0:T(2,128)(2,1)} %reshape.303), calls=%async_computation.3 | async-start | bytes 1048576 | tf_op jit(solution)/shard_map/all_to_all | solution.py:95
  101.0 28.1 %all-to-all-done.3 = bf16[128,2,1024]{2,1,0:T(2,128)(2,1)S(1)} async-done(((bf16[128,2,1024]{2,1,0:T(2,128)(2,1)}), bf16[128,2,1024]{2,1,0:T(2,128)(2,1)S(1)}, u32[]{:S(2)}, u32[]{:S(2)}) %all-to-all-start.3) | async-done | bytes 524320 | tf_op jit(solution)/shard_map/all_to_all | solution.py:95
  129.1 9.1 %all-to-all-start.4 = ((bf16[128,2,1024]{2,1,0:T(2,128)(2,1)}), bf16[128,2,1024]{2,1,0:T(2,128)(2,1)S(1)}, u32[]{:S(2)}, u32[]{:S(2)}) async-start(bf16[128,2,1024]{2,1,0:T(2,128)(2,1)} %reshape.305), calls=%async_computation.4 | async-start | bytes 1048576 | tf_op jit(solution)/shard_map/all_to_all | solution.py:98
  140.1 30.6 %all-to-all-done.4 = bf16[128,2,1024]{2,1,0:T(2,128)(2,1)S(1)} async-done(((bf16[128,2,1024]{2,1,0:T(2,128)(2,1)}), bf16[128,2,1024]{2,1,0:T(2,128)(2,1)S(1)}, u32[]{:S(2)}, u32[]{:S(2)}) %all-to-all-start.4) | async-done | bytes 524320 | tf_op jit(solution)/shard_map/all_to_all | solution.py:98
  170.7 10.2 %all-to-all-start.1 = ((bf16[128,2,1024]{2,1,0:T(2,128)(2,1)}), bf16[128,2,1024]{2,1,0:T(2,128)(2,1)S(1)}, u32[]{:S(2)}, u32[]{:S(2)}) async-start(bf16[128,2,1024]{2,1,0:T(2,128)(2,1)} %reshape.301), calls=%async_computation.1 | async-start | bytes 1048576 | tf_op jit(solution)/shard_map/all_to_all | solution.py:89
  182.9 30.2 %all-to-all-done.1 = bf16[128,2,1024]{2,1,0:T(2,128)(2,1)S(1)} async-done(((bf16[128,2,1024]{2,1,0:T(2,128)(2,1)}), bf16[128,2,1024]{2,1,0:T(2,128)(2,1)S(1)}, u32[]{:S(2)}, u32[]{:S(2)}) %all-to-all-start.1) | async-done | bytes 524320 | tf_op jit(solution)/shard_map/all_to_all | solution.py:89
  213.1 10.5 %all-to-all-start.2 = ((bf16[128,2,1024]{2,1,0:T(2,128)(2,1)}), bf16[128,2,1024]{2,1,0:T(2,128)(2,1)S(1)}, u32[]{:S(2)}, u32[]{:S(2)}) async-start(bf16[128,2,1024]{2,1,0:T(2,128)(2,1)} %reshape.299), calls=%async_computation.2 | async-start | bytes 1048576 | tf_op jit(solution)/shard_map/all_to_all | solution.py:92
  224.1 3.1 reduce.2
  228.3 3.1 reduce.3
  232.6 3.1 reduce
  236.4 23.9 %all-to-all-done.2 = bf16[128,2,1024]{2,1,0:T(2,128)(2,1)S(1)} async-done(((bf16[128,2,1024]{2,1,0:T(2,128)(2,1)}), bf16[128,2,1024]{2,1,0:T(2,128)(2,1)S(1)}, u32[]{:S(2)}, u32[]{:S(2)}) %all-to-all-start.2) | async-done | bytes 524320 | tf_op jit(solution)/shard_map/all_to_all | solution.py:92
  260.9 3.1 reduce.1
  275.3 9.1 %all-to-all-start.5 = ((bf16[2,128,1024]{2,0,1:T(2,128)(2,1)}), bf16[2,128,1024]{2,0,1:T(2,128)(2,1)S(1)}, u32[]{:S(2)}, u32[]{:S(2)}) async-start(bf16[2,128,1024]{2,0,1:T(2,128)(2,1)} %copy.35), calls=%async_computation.5 | async-start | bytes 1048576 | tf_op jit(solution)/shard_map/all_to_all | solution.py:113
  288.0 27.1 %all-to-all-done.5 = bf16[2,128,1024]{2,0,1:T(2,128)(2,1)S(1)} async-done(((bf16[2,128,1024]{2,0,1:T(2,128)(2,1)}), bf16[2,128,1024]{2,0,1:T(2,128)(2,1)S(1)}, u32[]{:S(2)}, u32[]{:S(2)}) %all-to-all-start.5) | async-done | bytes 524320 | tf_op jit(solution)/shard_map/all_to_all | solution.py:113
  315.1 9.6 %all-to-all-start.6 = ((bf16[2,128,1024]{2,0,1:T(2,128)(2,1)}), bf16[2,128,1024]{2,0,1:T(2,128)(2,1)}, u32[]{:S(2)}, u32[]{:S(2)}) async-start(bf16[2,128,1024]{2,0,1:T(2,128)(2,1)} %copy.36), calls=%async_computation.6 | async-start | bytes 1048576 | tf_op jit(solution)/shard_map/all_to_all | solution.py:116
  325.8 29.3 %all-to-all-done.6 = bf16[2,128,1024]{2,0,1:T(2,128)(2,1)} async-done(((bf16[2,128,1024]{2,0,1:T(2,128)(2,1)}), bf16[2,128,1024]{2,0,1:T(2,128)(2,1)}, u32[]{:S(2)}, u32[]{:S(2)}) %all-to-all-start.6) | async-done | bytes 524320 | tf_op jit(solution)/shard_map/all_to_all | solution.py:116
  355.1 1.4 convert_bitcast_fusion.1
  360.8 29.4 %all_to_all.108 = bf16[128,2,512]{2,1,0:T(2,128)(2,1)S(1)} all-to-all(bf16[128,2,512]{2,1,0:T(2,128)(2,1)S(1)} %reshape.307), channel_id=1, replica_groups=mesh['ctx'=128,'ch'=4] {'ctx'}, dimensions={0} | all-to-all | bytes 524288 | tf_op jit(solution)/shard_map/all_to_all | solution.py:125
  390.5 7.5 %convolution_convert_fusion = bf16[128,4096]{1,0:T(8,128)(2,1)} fusion(bf16[1024,4096]{0,1:T(8,128)(2,1)} %all-gather.2.cloned.1.call-done, f32[3,128,1024]{2,1,0:T(8,128)} %copy-done, f32[1,128,1024]{2,0,1:T(1,128)S(1)} %copy-done.1, bf16[128,1,1024]{2,1,0:T(2,128)(2,1)S(1)} %reshape.308, f32[1024]{0:T(1024)S(1)} %copy-done.4), kind=kOutput, calls=%fused_computation.6 | convolution fusion | flops 1074921472 | bytes 10752000 | tf_op jit(solution)/shard_map/dot_general | solution.py:129
  398.0 53.2 %all-reduce.2.cloned.1.call-done = bf16[128,4096]{1,0:T(8,128)(2,1)} async-done(((bf16[128,4096]{1,0:T(8,128)(2,1)}), bf16[128,4096]{1,0:T(8,128)(2,1)}) %all-reduce.2.cloned.1.call-update) | async-done | bytes 1048592 | tf_op jit(solution)/shard_map/psum | solution.py:134
  451.2 1.7 convert_convert_fusion
  (119 shorter events, 69.4 us)
Async XLA Ops:
  7.4 8.8 %collective-permute-start = (bf16[3,2,1024]{2,1,0:T(2,128)(2,1)S(1)}, bf16[3,2,1024]{2,1,0:T(2,128)(2,1)S(1)}, u32[]{:S(2)}, u32[]{:S(2)}) collective-permute-start(bf16[3,2,1024]{2,1,0:T(2,128)(2,1)S(1)} %slice.31), channel_id=1, source_target_pairs={{0,4},{4,8},{8,12},{12,16},{16,20},{20,24},{24,28},{28,32},{32,36}... | collective-permute-start | bytes 36872 | tf_op jit(solution)/shard_map/ppermute | solution.py:12
  18.0 1.2 copy-start
  24.2 51.1 %all-to-all-start = ((bf16[128,2,512]{2,1,0:T(2,128)(2,1)}), bf16[128,2,512]{2,1,0:T(2,128)(2,1)S(1)}, u32[]{:S(2)}, u32[]{:S(2)}) async-start(bf16[128,2,512]{2,1,0:T(2,128)(2,1)} %reshape.297), calls=%async_computation | async-start | bytes 524288 | tf_op jit(solution)/shard_map/all_to_all | solution.py:50
  79.1 19.8 %copy-start.3 = (bf16[256,1,1024]{2,0,1:T(8,128)(2,1)S(1)}, bf16[256,1,1024]{2,0,1:T(8,128)(2,1)}, u32[]{:S(2)}) copy-start(bf16[256,1,1024]{2,0,1:T(8,128)(2,1)} %get-tuple-element.135) | copy-start | bytes 1572868
  82.1 46.9 %all-to-all-start.3 = ((bf16[128,2,1024]{2,1,0:T(2,128)(2,1)}), bf16[128,2,1024]{2,1,0:T(2,128)(2,1)S(1)}, u32[]{:S(2)}, u32[]{:S(2)}) async-start(bf16[128,2,1024]{2,1,0:T(2,128)(2,1)} %reshape.303), calls=%async_computation.3 | async-start | bytes 1048576 | tf_op jit(solution)/shard_map/all_to_all | solution.py:95
  98.2 292.2 %all-gather.2.cloned.1.call-start = ((), (), s32[]{:S(2)}) async-start(), calls=%async_computation.8 | async-start | bytes 8454144 | tf_op jit(solution)/shard_map/all_gather | solution.py:131
  99.0 39.2 %copy-start.2 = (bf16[256,1,1024]{2,0,1:T(8,128)(2,1)S(1)}, bf16[256,1,1024]{2,0,1:T(8,128)(2,1)}, u32[]{:S(2)}) copy-start(bf16[256,1,1024]{2,0,1:T(8,128)(2,1)} %get-tuple-element.145) | copy-start | bytes 1572868
  129.1 41.7 %all-to-all-start.4 = ((bf16[128,2,1024]{2,1,0:T(2,128)(2,1)}), bf16[128,2,1024]{2,1,0:T(2,128)(2,1)S(1)}, u32[]{:S(2)}, u32[]{:S(2)}) async-start(bf16[128,2,1024]{2,1,0:T(2,128)(2,1)} %reshape.305), calls=%async_computation.4 | async-start | bytes 1048576 | tf_op jit(solution)/shard_map/all_to_all | solution.py:98
  170.7 42.3 %all-to-all-start.1 = ((bf16[128,2,1024]{2,1,0:T(2,128)(2,1)}), bf16[128,2,1024]{2,1,0:T(2,128)(2,1)S(1)}, u32[]{:S(2)}, u32[]{:S(2)}) async-start(bf16[128,2,1024]{2,1,0:T(2,128)(2,1)} %reshape.301), calls=%async_computation.1 | async-start | bytes 1048576 | tf_op jit(solution)/shard_map/all_to_all | solution.py:89
  213.1 47.2 %all-to-all-start.2 = ((bf16[128,2,1024]{2,1,0:T(2,128)(2,1)}), bf16[128,2,1024]{2,1,0:T(2,128)(2,1)S(1)}, u32[]{:S(2)}, u32[]{:S(2)}) async-start(bf16[128,2,1024]{2,1,0:T(2,128)(2,1)} %reshape.299), calls=%async_computation.2 | async-start | bytes 1048576 | tf_op jit(solution)/shard_map/all_to_all | solution.py:92
  275.3 39.8 %all-to-all-start.5 = ((bf16[2,128,1024]{2,0,1:T(2,128)(2,1)}), bf16[2,128,1024]{2,0,1:T(2,128)(2,1)S(1)}, u32[]{:S(2)}, u32[]{:S(2)}) async-start(bf16[2,128,1024]{2,0,1:T(2,128)(2,1)} %copy.35), calls=%async_computation.5 | async-start | bytes 1048576 | tf_op jit(solution)/shard_map/all_to_all | solution.py:113
  315.1 40.0 %all-to-all-start.6 = ((bf16[2,128,1024]{2,0,1:T(2,128)(2,1)}), bf16[2,128,1024]{2,0,1:T(2,128)(2,1)}, u32[]{:S(2)}, u32[]{:S(2)}) async-start(bf16[2,128,1024]{2,0,1:T(2,128)(2,1)} %copy.36), calls=%async_computation.6 | async-start | bytes 1048576 | tf_op jit(solution)/shard_map/all_to_all | solution.py:116
  324.6 126.5 %all-reduce.2.cloned.1.call-start = ((), (), s32[]{:S(2)}) async-start(), calls=%async_computation.9 | async-start | bytes 2097152 | tf_op jit(solution)/shard_map/psum | solution.py:134
  359.9 30.6 %copy-start.1 = (f32[1,128,1024]{2,0,1:T(1,128)S(1)}, f32[1,128,1024]{2,0,1:T(1,128)}, u32[]{:S(2)}) copy-start(f32[1,128,1024]{2,0,1:T(1,128)} %get-tuple-element.140) | copy-start | bytes 1572868
  359.9 30.6 %copy-start.4 = (f32[1024]{0:T(1024)S(1)}, f32[1024]{0:T(1024)}, u32[]{:S(2)}) copy-start(f32[1024]{0:T(1024)} %param.12) | copy-start | bytes 12292
Sparse Core Ops, SparseCore 0:
  102.2 169.9 all-gather.1
  398.1 53.0 all-reduce.1
where the time goes:
time: 467 us; the launch traced here: 460 us
  waiting for transfers between devices  225 us (48%)
  starting transfers between devices  86.9 us (19%)
  other arithmetic  57.5 us (12%)
  blocking collectives  29.4 us (6%)
  matrix products  28.4 us (6%)
  local copies, waits for them, and re-layouts  17.7 us (4%)
  between operations  14.2 us (3%)
    psum x1, waiting for transfers between devices, on_device(): total = lax.psum(partial_sum.astype(jnp.bfloat16), 'ch').astype(jnp.float32)  53.2 us
    all_to_all x1, waiting for transfers between devices, on_device(): lax.all_to_all(filter_imag.astype(jnp.bfloat16), 'ctx', split_axis=0, con...  30.6 us
    all_to_all x1, waiting for transfers between devices, on_device(): lax.all_to_all(first_real.astype(jnp.bfloat16), 'ctx', split_axis=0, conc...  30.2 us
    all_to_all x1, blocking collectives, on_device(): lax.all_to_all(rebuilt.astype(jnp.bfloat16), 'ctx', split_axis=0, concat_...  29.4 us
    all_to_all x1, waiting for transfers between devices, on_device(): lax.all_to_all(back_imag.astype(jnp.bfloat16), 'ctx', split_axis=1, conca...  29.3 us
    all_to_all x1, waiting for transfers between devices, on_device(): lax.all_to_all(filter_real.astype(jnp.bfloat16), 'ctx', split_axis=0, con...  28.1 us
    all_to_all x1, waiting for transfers between devices, on_device(): lax.all_to_all(back_real.astype(jnp.bfloat16), 'ctx', split_axis=1, conca...  27.1 us
    all_to_all x1, waiting for transfers between devices, on_device(): lax.all_to_all(first_imag.astype(jnp.bfloat16), 'ctx', split_axis=0, conc...  23.9 us
  transfers between devices with their start and end apart: 10, of which 8 were waited for; matrix products, arithmetic and copies ran while one was open for 17% of the time, Pallas kernels for 0%

commit v1 on v0

v1 whole, which is shorter than its diff:
```python
import functools

import jax
import jax.numpy as jnp
from jax import lax
from jax.experimental import pallas as pl
from jax.experimental.pallas import tpu as pltpu
from jax.sharding import PartitionSpec as P

MESH = pl.DeviceIdType.MESH
F32 = jnp.float32
BF16 = jnp.bfloat16
STEPS = 16
MODES = 16
BLOCKS = 8


def unit_offsets():
    order = [0]
    for k in range(1, 8):
        order += [-k, k]
    return order + [-8]


def kernel(
    proj, sfilt, res, dec, skip, wt, out,
    x32, lam_t, al_t, l16_t, l32_t, l64_t, taps_t, sf_t, l128_t, l2048_t, pow_t, z_t, q_t, u_t, y_t, gt,
    hal_s, hal_r, sb, ab, tb, bb, cs, cr, wbuf, gb, ps, rb,
    h_s, h_r, w_s, w_r, x2_r, xf_r, ph_s, ph_r, g_s, g_r, rs_s, rs_r,
):
    ctx = lax.axis_index("ctx")
    y = lax.axis_index("ch")
    z = ctx // 8
    x = (ctx // 2) % 4
    c = ctx % 2
    grp = ctx // 16
    g = ctx % 16
    sib = z * 8 + x * 2 + (1 - c)

    def at(zz, xx):
        return (zz % 16) * 8 + (xx % 4) * 2 + c

    zr, zl = at(z + 1, x), at(z + 15, x)
    xr, xl, xo = at(z, x + 1), at(z, x + 3), at(z, x + 2)
    nxt, prv = (ctx + 1) % 128, (ctx + 127) % 128

    barrier = pltpu.get_barrier_semaphore()

    def greet(who, chan):
        pl.semaphore_signal(barrier, inc=1, device_id=(who, chan), device_id_type=MESH)

    for d in range(1, 16):
        greet(grp * 16 + (g + d) % 16, y)
    for d in range(1, 8):
        greet(((grp + d) % 8) * 16 + g, y)
    for d in range(1, 4):
        greet(ctx, (y + d) % 4)
        greet(sib, (y + d) % 4)
    for who in (zr, zl, nxt, prv):
        greet(who, y)
    greetings = 15 + 7 + 6 + 4

    for b in range(3):
        rows = proj[b, 112:128, :].astype(F32)
        for l in range(BLOCKS):
            hal_s[l, 2 * b : 2 * b + 2, :] = rows[14:16, l * 128 : (l + 1) * 128]
    for l in range(BLOCKS):
        hal_s[l, 6:8, :] = jnp.zeros((2, 128), F32)
    me_slot = z * 4 + x
    wbuf[me_slot] = wt[...]
    row = lax.broadcasted_iota(jnp.int32, (8, 128), 0)
    chunk_start = row.astype(F32) * float(STEPS)

    for l in range(BLOCKS):
        lanes = slice(l * 128, (l + 1) * 128)
        for b in range(3):
            x32[b, l] = proj[b, :, lanes].astype(F32)
        rate = dec[:, lanes]
        lam_t[l] = jnp.exp(-rate)
        l16_t[l] = jnp.exp(-16.0 * rate)
        l32_t[l] = jnp.exp(-32.0 * rate)
        l64_t[l] = jnp.exp(-64.0 * rate)
        hop = jnp.exp(-128.0 * rate)
        far = jnp.exp(-2048.0 * rate)
        for half in range(2):
            l128_t[half * 8 + l] = hop[half * 8 : half * 8 + 8]
            l2048_t[half * 8 + l] = far[half * 8 : half * 8 + 8]
        for b in range(3):
            sf_t[l, 3 * b : 3 * b + 3, :] = sfilt[b, :, lanes]

    pl.semaphore_wait(barrier, greetings)

    def halo_copy():
        return pltpu.make_async_remote_copy(
            src_ref=hal_s, dst_ref=hal_r, send_sem=h_s, recv_sem=h_r,
            device_id=(nxt, y), device_id_type=MESH)

    halo_copy().start()

    def push(slot, who, sem):
        pltpu.make_async_remote_copy(
            src_ref=wbuf.at[slot], dst_ref=wbuf.at[slot], send_sem=w_s, recv_sem=sem,
            device_id=(who, y), device_id_type=MESH).start()

    def landed(slot, sem):
        pltpu.make_async_copy(wbuf.at[slot], wbuf.at[slot], sem).wait()

    order = unit_offsets()

    def spread(slot, offset):
        n = order.index(offset)
        push(slot, xr, xf_r.at[0, n])
        push(slot, xl, xf_r.at[1, n])

    push(me_slot, zr, w_r.at[0, 0])
    push(me_slot, zl, w_r.at[1, 0])
    push(me_slot, xo, x2_r)
    spread(me_slot, 0)

    def slot_of(offset, xx):
        return ((z + offset + 16) % 16) * 4 + (xx % 4)

    def relay(k):
        for way, (sign, onward, last) in enumerate(((-1, zr, 8), (1, zl, 7))):
            if k > last:
                continue
            own, other = slot_of(sign * k, x), slot_of(sign * k, x + 2)
            landed(own, w_r.at[way, k - 1])
            if k < last:
                push(own, onward, w_r.at[way, k])
            spread(own, sign * k)
            landed(other, w_r.at[2 + way, k - 1])
            if k < last:
                push(other, onward, w_r.at[2 + way, k])

    def tables(l, carry):
        rate = dec_block(l)
        lam = lam_t[l]
        amp = res_block(l) * jnp.sqrt(rate)
        al_t[l] = amp * lam
        weight = amp
        rows = []
        for tap in range(STEPS):
            rows.append(jnp.sum(weight, axis=0, keepdims=True))
            weight = weight * lam
        rows[0] = rows[0] + skip[:, pl.ds(pl.multiple_of(l * 128, 128), 128)]
        for tap in range(STEPS):
            taps_t[l, tap : tap + 1, :] = rows[tap]
        for m in range(MODES):
            pow_t[l, m] = jnp.exp(-chunk_start * rate[m : m + 1, :])
        return carry

    def dec_block(l):
        return dec[:, pl.ds(pl.multiple_of(l * 128, 128), 128)]

    def res_block(l):
        return res[:, pl.ds(pl.multiple_of(l * 128, 128), 128)]

    lax.fori_loop(0, BLOCKS, tables, 0)

    other = slot_of(0, x + 2)
    landed(other, x2_r)
    push(other, zr, w_r.at[2, 0])
    push(other, zl, w_r.at[3, 0])

    halo_copy().wait()
    known = jnp.where(ctx == 0, 0.0, 1.0).astype(F32)
    keep1 = jnp.where(row >= 1, 1.0, 0.0).astype(F32)
    keep2 = jnp.where(row >= 2, 1.0, 0.0).astype(F32)
    keep4 = jnp.where(row >= 4, 1.0, 0.0).astype(F32)

    def states(l, carry):
        halo = hal_r[l] * known
        filt = sf_t[l]
        shorts = []
        for b in range(3):
            xs = [x32[b, l, pl.ds(j, 8, stride=STEPS), :] for j in range(STEPS)]
            before1 = jnp.where(row >= 1, pltpu.roll(xs[15], 1, 0), halo[2 * b + 1 : 2 * b + 2, :])
            before2 = jnp.where(row >= 1, pltpu.roll(xs[14], 1, 0), halo[2 * b : 2 * b + 1, :])
            line = [before2, before1] + xs
            f0, f1, f2 = (filt[3 * b + i : 3 * b + i + 1, :] for i in range(3))
            shorts.append([f0 * line[j + 2] + f1 * line[j + 1] + f2 * line[j] for j in range(STEPS)])
        us = [(shorts[1][j] * shorts[2][j]).astype(BF16).astype(F32) for j in range(STEPS)]
        for j in range(STEPS):
            q_t[l, j] = shorts[0][j]
            u_t[l, j] = us[j]
        lam, l16, l32, l64 = lam_t[l], l16_t[l], l32_t[l], l64_t[l]
        for m in range(MODES):
            rate = jnp.broadcast_to(lam[m : m + 1, :], (8, 128))
            end = us[0]
            for j in range(1, STEPS):
                end = end * rate + us[j]
            end = end + pltpu.roll(end, 1, 0) * (keep1 * l16[m : m + 1, :])
            end = end + pltpu.roll(end, 2, 0) * (keep2 * l32[m : m + 1, :])
            end = end + pltpu.roll(end, 4, 0) * (keep4 * l64[m : m + 1, :])
            z_t[l, m] = pltpu.roll(end, 1, 0) * keep1
            sb[(m // 8) * 8 + l, m % 8 : m % 8 + 1, :] = end[7:8, :]
        return carry

    lax.fori_loop(0, 4, states, 0)
    relay(1)
    lax.fori_loop(4, 8, states, 0)

    def member(d):
        return (g + d) % 16

    def to_member(src, dst, d, k):
        pltpu.make_async_remote_copy(
            src_ref=src, dst_ref=dst, send_sem=ph_s.at[k], recv_sem=ph_r.at[k],
            device_id=(grp * 16 + member(d), y), device_id_type=MESH).start()

    ab[g] = sb[g]

    def send_a(d, carry):
        to_member(sb.at[member(d)], ab.at[g], d, 0)
        return carry

    lax.fori_loop(1, 16, send_a, 0)

    def local(l, carry):
        us = [u_t[l, j] for j in range(STEPS)]
        taps = taps_t[l]
        rows = [jnp.broadcast_to(taps[t : t + 1, :], (8, 128)) for t in range(STEPS)]
        for j in range(STEPS):
            total = rows[0] * us[j]
            for t in range(1, j + 1):
                total = total + rows[t] * us[j - t]
            y_t[l, j] = total
        return carry

    relay(2)
    lax.fori_loop(0, 4, local, 0)

    def group_wait(buf, count, k):
        part = buf.at[pl.ds(0, count)]
        pltpu.make_async_copy(part, part, ph_r.at[k]).wait()

    group_wait(ab, 15, 0)
    hop = l128_t[g]
    total = ab[0]
    for h in range(1, 16):
        total = total * hop + ab[h]
    tb[...] = total

    def send_b(d, carry):
        pltpu.make_async_remote_copy(
            src_ref=tb, dst_ref=bb.at[d - 1], send_sem=ph_s.at[1], recv_sem=ph_r.at[1],
            device_id=(((grp + d) % 8) * 16 + g, y), device_id_type=MESH).start()
        return carry

    lax.fori_loop(1, 8, send_b, 0)
    relay(3)
    lax.fori_loop(4, 8, local, 0)
    group_wait(bb, 7, 1)
    far = l2048_t[g]
    state = jnp.zeros((8, 128), F32)
    for d in range(7, 0, -1):
        state = state * far + bb[d - 1] * jnp.where(grp >= d, 1.0, 0.0).astype(F32)
    for h in range(16):
        cs[h] = state
        state = state * hop + ab[h]
    cr[g] = cs[g]

    def send_c(d, carry):
        to_member(cs.at[member(d)], cr.at[g], d, 2)
        return carry

    lax.fori_loop(1, 16, send_c, 0)
    relay(4)
    group_wait(cr, 15, 2)

    def finish(l, carry):
        ys = [y_t[l, j] for j in range(STEPS)]
        lam, al = lam_t[l], al_t[l]
        tiles = [cr[l], cr[8 + l]]
        for m in range(MODES):
            rate = jnp.broadcast_to(lam[m : m + 1, :], (8, 128))
            start = z_t[l, m] + pow_t[l, m] * tiles[m // 8][m % 8 : m % 8 + 1, :]
            term = start * al[m : m + 1, :]
            for j in range(STEPS):
                ys[j] = ys[j] + term
                if j < STEPS - 1:
                    term = term * rate
        for j in range(STEPS):
            gt[l, pl.ds(j, 8, stride=STEPS), :] = q_t[l, j] * ys[j]
        return carry

    lax.fori_loop(0, 4, finish, 0)
    relay(5)
    lax.fori_loop(4, 8, finish, 0)
    for l in range(BLOCKS):
        gb[0, :, l * 128 : (l + 1) * 128] = gt[l].astype(BF16)
    gated = pltpu.make_async_remote_copy(
        src_ref=gb.at[0], dst_ref=gb.at[1], send_sem=g_s, recv_sem=g_r,
        device_id=(sib, y), device_id_type=MESH)
    gated.start()
    relay(6)
    gated.wait()

    def unit(n):
        offset = order[n]
        zq = (z + offset + 16) % 16
        landed(zq * 4 + (x + 3) % 4, xf_r.at[0, n])
        landed(zq * 4 + (x + 1) % 4, xf_r.at[1, n])
        weights = wbuf[pl.ds(zq * 4, 4)].reshape(128, 1024)
        part = lax.dot_general(
            gb[...].reshape(256, 1024), weights, (((1,), (1,)), ((), ())),
            preferred_element_type=F32).astype(BF16)
        ps[2 * n] = part[:128]
        ps[2 * n + 1] = part[128:]
        owner, place = zq // 4, zq % 4
        dy = (owner - y + 4) % 4
        pltpu.make_async_remote_copy(
            src_ref=ps.at[2 * n + 1], dst_ref=rb.at[dy, 1, place], send_sem=rs_s,
            recv_sem=rs_r.at[dy, 1, place], device_id=(sib, owner), device_id_type=MESH).start()

        @pl.when(dy != 0)
        def _():
            pltpu.make_async_remote_copy(
                src_ref=ps.at[2 * n], dst_ref=rb.at[dy, 0, place], send_sem=rs_s,
                recv_sem=rs_r.at[dy, 0, place], device_id=(ctx, owner), device_id_type=MESH).start()

        @pl.when(dy == 0)
        def _():
            rb[0, 0, place] = ps[2 * n]

    for n in range(0, 9):
        unit(n)
    relay(7)
    for n in range(9, 13):
        unit(n)
    relay(8)
    for n in range(13, 16):
        unit(n)

    lane = lax.broadcasted_iota(jnp.int32, (128, 128), 1) // 32
    for place in range(4):
        sums = []
        for core in range(2):
            rel = (core + c) % 2
            for dy in range(4):
                if core == 0:
                    for r in range(2):
                        if dy or r:
                            pltpu.make_async_copy(
                                rb.at[dy, r, place], rb.at[dy, r, place], rs_r.at[dy, r, place]).wait()
            acc = rb[0, rel, place].astype(F32)
            for dy in range(1, 4):
                acc = acc + rb[dy, rel, place].astype(F32)
            sums.append(acc)
        a, b = sums

        def pick(parts):
            return jnp.where(lane == 0, parts[0], jnp.where(lane == 1, parts[1], jnp.where(lane == 2, parts[2], parts[3])))

        a32, a64, a96 = (pltpu.roll(a, s, 1) for s in (32, 64, 96))
        b32, b64, b96 = (pltpu.roll(b, s, 1) for s in (32, 64, 96))
        out[:, place * 256 : place * 256 + 128] = pick((a, b32, a32, b64)).astype(BF16)
        out[:, place * 256 + 128 : place * 256 + 256] = pick((a64, b96, a96, b)).astype(BF16)

    part = wbuf.at[pl.ds(0, 63)]
    pltpu.make_async_copy(part, part, w_s).wait()
    for k, (buf, count) in enumerate(((sb, 15), (bb, 7), (cs, 15))):
        part = buf.at[pl.ds(0, count)]
        pltpu.make_async_copy(part, part, ph_s.at[k]).wait()
    part = ps.at[pl.ds(0, 28)]
    pltpu.make_async_copy(part, part, rs_s).wait()


def on_device(projected, short_filter, residues, decays, skip, out_weight):
    tile = (BLOCKS, MODES, 128)
    vm = pltpu.VMEM
    dma = pltpu.SemaphoreType.DMA
    return pl.pallas_call(
        kernel,
        out_shape=jax.ShapeDtypeStruct((128, 1024), BF16),
        in_specs=[pl.BlockSpec(memory_space=pltpu.VMEM)] * 6,
        out_specs=pl.BlockSpec(memory_space=pltpu.VMEM),
        scratch_shapes=[
            vm((3, 8, 128, 128), F32),
            vm(tile, F32), vm(tile, F32), vm(tile, F32), vm(tile, F32), vm(tile, F32),
            vm(tile, F32), vm(tile, F32),
            vm((16, 8, 128), F32), vm((16, 8, 128), F32),
            vm((8, 16, 8, 128), F32), vm((8, 16, 8, 128), F32),
            vm((8, 16, 8, 128), F32), vm((8, 16, 8, 128), F32), vm((8, 16, 8, 128), F32),
            vm((8, 128, 128), F32),
            vm((8, 8, 128), F32), vm((8, 8, 128), F32),
            vm((16, 8, 128), F32), vm((16, 8, 128), F32), vm((8, 128), F32),
            vm((8, 8, 128), F32), vm((16, 8, 128), F32), vm((16, 8, 128), F32),
            vm((64, 32, 1024), BF16), vm((2, 128, 1024), BF16),
            vm((32, 128, 128), BF16), vm((4, 2, 4, 128, 128), BF16),
            dma, dma, dma, dma((4, 8)), dma, dma((2, 16)), dma((3,)), dma((3,)),
            dma, dma, dma, dma((4, 2, 4)),
        ],
        compiler_params=pltpu.CompilerParams(
            collective_id=0, has_side_effects=True, vmem_limit_bytes=40 * 2**20),
        cost_estimate=pl.CostEstimate(flops=2**31, bytes_accessed=2**21, transcendentals=2**18),
        name="hyena",
    )(projected, short_filter, residues.T, decays.T, skip[None, :], out_weight.T)


def solution(mesh):
    return jax.shard_map(
        on_device,
        mesh=mesh,
        in_specs=(
            P(None, "ctx", "ch"), P(None, None, "ch"), P("ch", None), P("ch", None), P("ch"), P("ch", "ctx"),
        ),
        out_specs=P("ctx", "ch"),
        check_vma=False,
    )
```

time: 467 us -> 72.6 us (0.16)
  the two profiles are of different devices: /device:TPU:1 before, /device:TPU:16 now
where the time goes in v1:
time: 72.6 us; the launch traced here: 72.2 us
  Pallas kernels  66.4 us (91%)
  local copies, waits for them, and re-layouts  5.84 us (8%)
    pallas_call x1, Pallas kernels, on_device(): pl.pallas_call(kernel, out_shape=jax.ShapeDtypeStruct((128, 1024), BF16),...  66.4 us
    unnamed x13, local copies, waits for them, and re-layouts  5.84 us

profile of v1, /device:TPU:16, one launch (start us, length us, event | category | flops | bytes accessed | tf_op | source)
XLA Modules:
  0.0 72.2 jit_solution(17985596487707195533)
XLA Ops:
  0.0 0.0 copy-start.5
  0.0 0.7 copy-done.5
  0.7 0.0 copy-start
  0.7 1.1 %copy-done = bf16[3,128,1024]{2,1,0:T(8,128)(2,1)S(1)} copy-done((bf16[3,128,1024]{2,1,0:T(8,128)(2,1)S(1)}, bf16[3,128,1024]{2,1,0:T(8,128)(2,1)}, u32[]{:S(2)}) %copy-start) | copy-done | bytes 786456
  1.8 0.0 copy-start.1
  1.8 0.8 %copy-done.1 = f32[1024,16]{0,1:T(8,128)S(1)} copy-done((f32[1024,16]{0,1:T(8,128)S(1)}, f32[1024,16]{0,1:T(8,128)}, u32[]{:S(2)}) %copy-start.1) | copy-done | bytes 65560
  2.7 0.0 copy-start.2
  2.7 0.8 %copy-done.2 = f32[1024,16]{0,1:T(8,128)S(1)} copy-done((f32[1024,16]{0,1:T(8,128)S(1)}, f32[1024,16]{0,1:T(8,128)}, u32[]{:S(2)}) %copy-start.2) | copy-done | bytes 65560
  3.5 0.0 copy-start.3
  3.5 0.8 %copy-done.3 = bf16[1024,32]{0,1:T(8,128)(2,1)S(1)} copy-done((bf16[1024,32]{0,1:T(8,128)(2,1)S(1)}, bf16[1024,32]{0,1:T(8,128)(2,1)}, u32[]{:S(2)}) %copy-start.3) | copy-done | bytes 65560
  4.3 0.0 copy-start.4
  4.3 0.8 %copy-done.4 = f32[3,3,1024]{2,1,0:T(4,128)S(1)} copy-done((f32[3,3,1024]{2,1,0:T(4,128)S(1)}, f32[3,3,1024]{2,1,0:T(4,128)}, u32[]{:S(2)}) %copy-start.4) | copy-done | bytes 36888
  5.1 66.4 %hyena.1 = bf16[128,1024]{1,0:T(8,128)(2,1)S(1)} custom-call(bf16[3,128,1024]{2,1,0:T(8,128)(2,1)S(1)} %copy-done, f32[3,3,1024]{2,1,0:T(4,128)S(1)} %copy-done.4, f32[16,1024]{1,0:T(8,128)S(1)} %bitcast.4, f32[16,1024]{1,0:T(8,128)S(1)} %bitcast.5, f32[1,1024]{1,0:T(1,128)S(1)} %bitcast.7, bf16[32,1024]{1,0:T(8,128)(2,1)S(1)} %bitcast.6), custom_call_target="tpu_custom_call" | custom-call | flops 2147483648 | bytes 2097152 | tf_op jit(solution)/shard_map/hyena/pallas_call | solution.py:374
  71.5 0.7 copy.8
Async XLA Ops:
  0.0 0.7 copy-start.5
  0.7 1.1 %copy-start = (bf16[3,128,1024]{2,1,0:T(8,128)(2,1)S(1)}, bf16[3,128,1024]{2,1,0:T(8,128)(2,1)}, u32[]{:S(2)}) copy-start(bf16[3,128,1024]{2,1,0:T(8,128)(2,1)} %proj.1) | copy-start | bytes 2359300
  1.8 0.8 %copy-start.1 = (f32[1024,16]{0,1:T(8,128)S(1)}, f32[1024,16]{0,1:T(8,128)}, u32[]{:S(2)}) copy-start(f32[1024,16]{0,1:T(8,128)} %param.8) | copy-start | bytes 196612
  2.7 0.8 %copy-start.2 = (f32[1024,16]{0,1:T(8,128)S(1)}, f32[1024,16]{0,1:T(8,128)}, u32[]{:S(2)}) copy-start(f32[1024,16]{0,1:T(8,128)} %param.9) | copy-start | bytes 196612
  3.5 0.8 %copy-start.3 = (bf16[1024,32]{0,1:T(8,128)(2,1)S(1)}, bf16[1024,32]{0,1:T(8,128)(2,1)}, u32[]{:S(2)}) copy-start(bf16[1024,32]{0,1:T(8,128)(2,1)} %param.11) | copy-start | bytes 196612
  4.3 0.8 %copy-start.4 = (f32[3,3,1024]{2,1,0:T(4,128)S(1)}, f32[3,3,1024]{2,1,0:T(4,128)}, u32[]{:S(2)}) copy-start(f32[3,3,1024]{2,1,0:T(4,128)} %sfilt.1) | copy-start | bytes 110596

commit v2 on v1

--- a/solution.py
+++ b/solution.py
@@ -12,6 +12,8 @@
 BF16 = jnp.bfloat16
 STEPS = 16
 MODES = 16
+OWN = 2
+OTHER = 2
 BLOCKS = 8
 
 
@@ -23,10 +25,11 @@
 
 
 def kernel(
-    proj, sfilt, res, dec, skip, wt, out,
+    proj_h, sfilt_h, res_h, dec_h, skip_h, wt, out,
+    proj, sfilt, res, dec, skip,
     x32, lam_t, al_t, l16_t, l32_t, l64_t, taps_t, sf_t, l128_t, l2048_t, pow_t, z_t, q_t, u_t, y_t, gt,
     hal_s, hal_r, sb, ab, tb, bb, cs, cr, wbuf, gb, ps, rb,
-    h_s, h_r, w_s, w_r, x2_r, xf_r, ph_s, ph_r, g_s, g_r, rs_s, rs_r,
+    in_s, h_s, h_r, w_s, w_r, x2_r, xf_r, ph_s, ph_r, g_s, g_r, rs_s, rs_r, st,
 ):
     ctx = lax.axis_index("ctx")
     y = lax.axis_index("ch")
@@ -44,33 +47,114 @@
     xr, xl, xo = at(z, x + 1), at(z, x + 3), at(z, x + 2)
     nxt, prv = (ctx + 1) % 128, (ctx + 127) % 128
 
+    me_slot = z * 4 + x
+
+    def fetch(k, src, dst):
+        return pltpu.make_async_copy(src, dst, in_s.at[k])
+
+    fetches = [
+        fetch(0, proj_h, proj), fetch(1, wt, wbuf.at[me_slot]), fetch(2, dec_h, dec),
+        fetch(3, sfilt_h, sfilt), fetch(4, res_h, res), fetch(5, skip_h, skip),
+    ]
+    for copy in fetches:
+        copy.start()
+
     barrier = pltpu.get_barrier_semaphore()
 
     def greet(who, chan):
         pl.semaphore_signal(barrier, inc=1, device_id=(who, chan), device_id_type=MESH)
 
+    beyond = at(z + 1 - 2 * ((z + 1) % 2) + 16, x)
+    for who in (beyond, prv, at(z + 2, x), at(z + 14, x)):
+        greet(who, y)
     for d in range(1, 16):
         greet(grp * 16 + (g + d) % 16, y)
-    for d in range(1, 8):
-        greet(((grp + d) % 8) * 16 + g, y)
     for d in range(1, 4):
         greet(ctx, (y + d) % 4)
         greet(sib, (y + d) % 4)
-    for who in (zr, zl, nxt, prv):
-        greet(who, y)
-    greetings = 15 + 7 + 6 + 4
-
+    greetings = 4 + 15 + 6
+
+    fetches[0].wait()
     for b in range(3):
         rows = proj[b, 112:128, :].astype(F32)
         for l in range(BLOCKS):
             hal_s[l, 2 * b : 2 * b + 2, :] = rows[14:16, l * 128 : (l + 1) * 128]
     for l in range(BLOCKS):
         hal_s[l, 6:8, :] = jnp.zeros((2, 128), F32)
-    me_slot = z * 4 + x
-    wbuf[me_slot] = wt[...]
     row = lax.broadcasted_iota(jnp.int32, (8, 128), 0)
     chunk_start = row.astype(F32) * float(STEPS)
-
+    fetches[1].wait()
+    pl.semaphore_wait(barrier, greetings)
+
+    def tell(k, far):
+        for step in (far, 16 - far):
+            pl.semaphore_signal(st.at[k], inc=1, device_id=(at(z + step, x), y), device_id_type=MESH)
+
+
+    def halo_copy():
+        return pltpu.make_async_remote_copy(
+            src_ref=hal_s, dst_ref=hal_r, send_sem=h_s, recv_sem=h_r,
+            device_id=(nxt, y), device_id_type=MESH)
+
+    halo_copy().start()
+
+    def rows_of(slot, part, parts):
+        size = 32 // parts
+        return wbuf.at[slot, pl.ds(part * size, size)]
+
+    def push(slot, part, parts, who, sem):
+        block = rows_of(slot, part, parts)
+        pltpu.make_async_remote_copy(
+            src_ref=block, dst_ref=block, send_sem=w_s, recv_sem=sem,
+            device_id=(who, y), device_id_type=MESH).start()
+
+    def landed(slot, part, parts, sem):
+        block = rows_of(slot, part, parts)
+        pltpu.make_async_copy(block, block, sem).wait()
+
+    order = unit_offsets()
+
+    def spread(slot, offset, part):
+        n = order.index(offset)
+        push(slot, part, OWN, xr, xf_r.at[0, n, part])
+        push(slot, part, OWN, xl, xf_r.at[1, n, part])
+
+    def slot_of(offset, xx):
+        return ((z + offset + 16) % 16) * 4 + (xx % 4)
+
+    ways = ((-1, zr, 8), (1, zl, 7))
+    for part in range(OWN):
+        for way in range(2):
+            push(me_slot, part, OWN, ways[way][1], w_r.at[way, 0, part])
+    for part in range(OTHER):
+        push(me_slot, part, OTHER, xo, x2_r.at[part])
+    for part in range(OWN):
+        spread(me_slot, 0, part)
+    tell(0, 2)
+
+    def relay_own(k):
+        for part in range(OWN):
+            for way, (sign, onward, last) in enumerate(ways):
+                if k <= last:
+                    slot = slot_of(sign * k, x)
+                    landed(slot, part, OWN, w_r.at[way, k - 1, part])
+                    if k < last:
+                        push(slot, part, OWN, onward, w_r.at[way, k, part])
+            for sign, _, last in ways:
+                if k <= last:
+                    spread(slot_of(sign * k, x), sign * k, part)
+
+    def relay_other(k):
+        for part in range(OTHER):
+            for way, (sign, onward, last) in enumerate(ways):
+                if k <= last:
+                    slot = slot_of(sign * k, x + 2)
+                    landed(slot, part, OTHER, w_r.at[2 + way, k - 1, part])
+                    if k < last:
+                        push(slot, part, OTHER, onward, w_r.at[2 + way, k, part])
+
+    for copy in fetches[2:]:
+        copy.wait()
     for l in range(BLOCKS):
         lanes = slice(l * 128, (l + 1) * 128)
         for b in range(3):
@@ -88,51 +172,6 @@
         for b in range(3):
             sf_t[l, 3 * b : 3 * b + 3, :] = sfilt[b, :, lanes]
 
-    pl.semaphore_wait(barrier, greetings)
-
-    def halo_copy():
-        return pltpu.make_async_remote_copy(
-            src_ref=hal_s, dst_ref=hal_r, send_sem=h_s, recv_sem=h_r,
-            device_id=(nxt, y), device_id_type=MESH)
-
-    halo_copy().start()
-
-    def push(slot, who, sem):
-        pltpu.make_async_remote_copy(
-            src_ref=wbuf.at[slot], dst_ref=wbuf.at[slot], send_sem=w_s, recv_sem=sem,
-            device_id=(who, y), device_id_type=MESH).start()
-
-    def landed(slot, sem):
-        pltpu.make_async_copy(wbuf.at[slot], wbuf.at[slot], sem).wait()
-
-    order = unit_offsets()
-
-    def spread(slot, offset):
-        n = order.index(offset)
-        push(slot, xr, xf_r.at[0, n])
-        push(slot, xl, xf_r.at[1, n])
-
-    push(me_slot, zr, w_r.at[0, 0])
-    push(me_slot, zl, w_r.at[1, 0])
-    push(me_slot, xo, x2_r)
-    spread(me_slot, 0)
-
-    def slot_of(offset, xx):
-        return ((z + offset + 16) % 16) * 4 + (xx % 4)
-
-    def relay(k):
-        for way, (sign, onward, last) in enumerate(((-1, zr, 8), (1, zl, 7))):
-            if k > last:
-                continue
-            own, other = slot_of(sign * k, x), slot_of(sign * k, x + 2)
-            landed(own, w_r.at[way, k - 1])
-            if k < last:
-                push(own, onward, w_r.at[way, k])
-            spread(own, sign * k)
-            landed(other, w_r.at[2 + way, k - 1])
-            if k < last:
-                push(other, onward, w_r.at[2 + way, k])
-
     def tables(l, carry):
         rate = dec_block(l)
         lam = lam_t[l]
@@ -156,12 +195,11 @@
     def res_block(l):
         return res[:, pl.ds(pl.multiple_of(l * 128, 128), 128)]
 
-    lax.fori_loop(0, BLOCKS, tables, 0)
-
     other = slot_of(0, x + 2)
-    landed(other, x2_r)
-    push(other, zr, w_r.at[2, 0])
-    push(other, zl, w_r.at[3, 0])
+    for part in range(OTHER):
+        landed(other, part, OTHER, x2_r.at[part])
+        push(other, part, OTHER, zr, w_r.at[2, 0, part])
+        push(other, part, OTHER, zl, w_r.at[3, 0, part])
 
     halo_copy().wait()
     known = jnp.where(ctx == 0, 0.0, 1.0).astype(F32)
@@ -198,7 +236,9 @@
         return carry
 
     lax.fori_loop(0, 4, states, 0)
-    relay(1)
+    relay_own(1)
+    pl.semaphore_wait(st.at[0], 2)
+    tell(1, 4)
     lax.fori_loop(4, 8, states, 0)
 
     def member(d):
@@ -228,8 +268,11 @@
             y_t[l, j] = total
         return carry
 
-    relay(2)
-    lax.fori_loop(0, 4, local, 0)
+    relay_other(1)
+    lax.fori_loop(0, BLOCKS, tables, 0)
+    relay_own(2)
+    lax.fori_loop(0, 8, local, 0)
+    relay_other(2)
 
     def group_wait(buf, count, k):
         part = buf.at[pl.ds(0, count)]
@@ -248,9 +291,12 @@
             device_id=(((grp + d) % 8) * 16 + g, y), device_id_type=MESH).start()
         return carry
 
+    pl.semaphore_wait(st.at[1], 2)
     lax.fori_loop(1, 8, send_b, 0)
-    relay(3)
-    lax.fori_loop(4, 8, local, 0)
+    relay_own(3)
+    relay_other(3)
+    relay_own(4)
+    relay_other(4)
     group_wait(bb, 7, 1)
     far = l2048_t[g]
     state = jnp.zeros((8, 128), F32)
@@ -266,7 +312,8 @@
         return carry
 
     lax.fori_loop(1, 16, send_c, 0)
-    relay(4)
+    relay_own(5)
+    relay_other(5)
     group_wait(cr, 15, 2)
 
     def finish(l, carry):
@@ -285,29 +332,43 @@
             gt[l, pl.ds(j, 8, stride=STEPS), :] = q_t[l, j] * ys[j]
         return carry
 
-    lax.fori_loop(0, 4, finish, 0)
-    relay(5)
-    lax.fori_loop(4, 8, finish, 0)
-    for l in range(BLOCKS):
-        gb[0, :, l * 128 : (l + 1) * 128] = gt[l].astype(BF16)
-    gated = pltpu.make_async_remote_copy(
-        src_ref=gb.at[0], dst_ref=gb.at[1], send_sem=g_s, recv_sem=g_r,
-        device_id=(sib, y), device_id_type=MESH)
-    gated.start()
-    relay(6)
-    gated.wait()
-
-    def unit(n):
-        offset = order[n]
-        zq = (z + offset + 16) % 16
-        landed(zq * 4 + (x + 3) % 4, xf_r.at[0, n])
-        landed(zq * 4 + (x + 1) % 4, xf_r.at[1, n])
-        weights = wbuf[pl.ds(zq * 4, 4)].reshape(128, 1024)
+    def gated(half):
+        lanes = pl.ds(half * 512, 512)
+        return pltpu.make_async_remote_copy(
+            src_ref=gb.at[0, :, lanes], dst_ref=gb.at[1, :, lanes], send_sem=g_s.at[half],
+            recv_sem=g_r.at[half], device_id=(sib, y), device_id_type=MESH)
+
+    for half in range(2):
+        lax.fori_loop(4 * half, 4 * half + 4, finish, 0)
+        for l in range(4 * half, 4 * half + 4):
+            gb[0, :, l * 128 : (l + 1) * 128] = gt[l].astype(BF16)
+        gated(half).start()
+        if half == 0:
+            relay_own(6)
+    for half in range(2):
+        gated(half).wait()
+    relay_other(6)
+
+    def units(*offsets):
+        weights = []
+        for offset in offsets:
+            n = order.index(offset)
+            zq = (z + offset + 16) % 16
+            for part in range(OWN):
+                landed(zq * 4 + (x + 3) % 4, part, OWN, xf_r.at[0, n, part])
+                landed(zq * 4 + (x + 1) % 4, part, OWN, xf_r.at[1, n, part])
+            weights.append(wbuf[pl.ds(zq * 4, 4)].reshape(128, 1024))
         part = lax.dot_general(
-            gb[...].reshape(256, 1024), weights, (((1,), (1,)), ((), ())),
+            gb[...].reshape(256, 1024), jnp.concatenate(weights, axis=0), (((1,), (1,)), ((), ())),
             preferred_element_type=F32).astype(BF16)
-        ps[2 * n] = part[:128]
-        ps[2 * n + 1] = part[128:]
+        for i, offset in enumerate(offsets):
+            n = order.index(offset)
+            zq = (z + offset + 16) % 16
+            ps[2 * n] = part[:128, i * 128 : (i + 1) * 128]
+            ps[2 * n + 1] = part[128:, i * 128 : (i + 1) * 128]
+            ship(n, zq)
+
+    def ship(n, zq):
         owner, place = zq // 4, zq % 4
         dy = (owner - y + 4) % 4
         pltpu.make_async_remote_copy(
@@ -324,14 +385,19 @@
         def _():
             rb[0, 0, place] = ps[2 * n]
 
-    for n in range(0, 9):
-        unit(n)
-    relay(7)
-    for n in range(9, 13):
-        unit(n)
-    relay(8)
-    for n in range(13, 16):
-        unit(n)
+    units(0, 4)
+    units(-4, 1)
+    units(5, -3)
+    relay_own(7)
+    units(-1, 3)
+    units(-5, 2)
+    relay_other(7)
+    units(6, -2)
+    relay_own(8)
+    units(-6, 7)
+    relay_other(8)
+    units(-7)
+    units(-8)
 
     lane = lax.broadcasted_iota(jnp.int32, (128, 128), 1) // 32
     for place in range(4):
@@ -374,9 +440,10 @@
     return pl.pallas_call(
         kernel,
         out_shape=jax.ShapeDtypeStruct((128, 1024), BF16),
-        in_specs=[pl.BlockSpec(memory_space=pltpu.VMEM)] * 6,
+        in_specs=[pl.BlockSpec(memory_space=pl.ANY)] * 6,
         out_specs=pl.BlockSpec(memory_space=pltpu.VMEM),
         scratch_shapes=[
+            vm((3, 128, 1024), BF16), vm((3, 3, 1024), F32), vm((16, 1024), F32), vm((16, 1024), F32), vm((1, 1024), F32),
             vm((3, 8, 128, 128), F32),
             vm(tile, F32), vm(tile, F32), vm(tile, F32), vm(tile, F32), vm(tile, F32),
             vm(tile, F32), vm(tile, F32),
@@ -389,11 +456,11 @@
             vm((8, 8, 128), F32), vm((16, 8, 128), F32), vm((16, 8, 128), F32),
             vm((64, 32, 1024), BF16), vm((2, 128, 1024), BF16),
             vm((32, 128, 128), BF16), vm((4, 2, 4, 128, 128), BF16),
-            dma, dma, dma, dma((4, 8)), dma, dma((2, 16)), dma((3,)), dma((3,)),
-            dma, dma, dma, dma((4, 2, 4)),
+            dma((6,)), dma, dma, dma, dma((4, 8, 2)), dma((2,)), dma((2, 16, 2)), dma((3,)), dma((3,)),
+            dma((2,)), dma((2,)), dma, dma((4, 2, 4)), pltpu.SemaphoreType.REGULAR((2,)),
         ],
         compiler_params=pltpu.CompilerParams(
-            collective_id=0, has_side_effects=True, vmem_limit_bytes=40 * 2**20),
+            collective_id=0, has_side_effects=True, vmem_limit_bytes=63 * 2**20),
         cost_estimate=pl.CostEstimate(flops=2**31, bytes_accessed=2**21, transcendentals=2**18),
         name="hyena",
     )(projected, short_filter, residues.T, decays.T, skip[None, :], out_weight.T)

time: 72.6 us -> 62.2 us (0.86)
  the two profiles are of different devices: /device:TPU:16 before, /device:TPU:48 now
where the time goes in v2:
time: 62.2 us; the launch traced here: 62 us
  Pallas kernels  60.4 us (97%)
  local copies, waits for them, and re-layouts  1.67 us (3%)
    pallas_call x1, Pallas kernels, on_device(): pl.pallas_call(kernel, out_shape=jax.ShapeDtypeStruct((128, 1024), BF16),...  60.4 us
    unnamed x1, local copies, waits for them, and re-layouts  1.67 us

profile of v2, /device:TPU:48, one launch (start us, length us, event | category | flops | bytes accessed | tf_op | source)
XLA Modules:
  0.0 62.0 jit_solution(7812249757541010077)
XLA Ops:
  0.0 60.4 %hyena.1 = bf16[128,1024]{1,0:T(8,128)(2,1)} custom-call(bf16[3,128,1024]{2,1,0:T(8,128)(2,1)} %proj_h.1, f32[3,3,1024]{2,1,0:T(4,128)} %sfilt_h.1, f32[16,1024]{1,0:T(8,128)} %bitcast.4, f32[16,1024]{1,0:T(8,128)} %bitcast.5, f32[1,1024]{1,0:T(1,128)} %bitcast.7, bf16[32,1024]{1,0:T(8,128)(2,1)} %bitcast.6), custom_call_target="tpu_custom_call" | custom-call | flops 2147483648 | bytes 2097152 | tf_op jit(solution)/shard_map/hyena/pallas_call | solution.py:440
  60.4 1.7 %copy.8 = bf16[128,1024]{1,0:T(8,128)(2,1)} copy(bf16[128,1024]{1,0:T(8,128)(2,1)} %hyena.1) | data formatting | bytes 524288

commit v3 on v2

--- a/solution.py
+++ b/solution.py
@@ -17,11 +17,12 @@
 BLOCKS = 8
 
 
-def unit_offsets():
-    order = [0]
-    for k in range(1, 8):
-        order += [-k, k]
-    return order + [-8]
+TURNS = (
+    (-5, 4, 0, -4, 5, 1, -6, 6, -3, 2, -7, 7, -2, 3, -1, -8),
+    (4, -5, 0, -4, 5, 1, -6, 6, 3, -1, 7, -7, -3, 2, -2, -8),
+    (5, -4, 0, 4, -5, 1, 6, -6, 3, -1, 7, -7, -3, 2, -2, -8),
+    (5, -4, 4, 0, -5, -1, 6, -6, 3, -2, 7, -7, 2, -3, 1, -8),
+)
 
 
 def kernel(
@@ -49,6 +50,14 @@
 
     me_slot = z * 4 + x
 
+    barrier = pltpu.get_barrier_semaphore()
+    twin = at(z + 1 - 2 * (z % 2) + 16, x)
+    near = (zr, zl, xr, xl, xo, sib, prv, twin + 1 - 2 * c, at(z + 2, x), at(z + 14, x))
+    for who in near:
+        pl.semaphore_signal(barrier, inc=1, device_id=(who, y), device_id_type=MESH)
+    for d in range(1, 4):
+        pl.semaphore_signal(barrier, inc=1, device_id=(ctx, (y + d) % 4), device_id_type=MESH)
+
     def fetch(k, src, dst):
         return pltpu.make_async_copy(src, dst, in_s.at[k])
 
@@ -59,20 +68,55 @@
     for copy in fetches:
         copy.start()
 
-    barrier = pltpu.get_barrier_semaphore()
-
-    def greet(who, chan):
-        pl.semaphore_signal(barrier, inc=1, device_id=(who, chan), device_id_type=MESH)
-
-    beyond = at(z + 1 - 2 * ((z + 1) % 2) + 16, x)
-    for who in (beyond, prv, at(z + 2, x), at(z + 14, x)):
-        greet(who, y)
-    for d in range(1, 16):
-        greet(grp * 16 + (g + d) % 16, y)
-    for d in range(1, 4):
-        greet(ctx, (y + d) % 4)
-        greet(sib, (y + d) % 4)
-    greetings = 4 + 15 + 6
+    row = lax.broadcasted_iota(jnp.int32, (8, 128), 0)
+    chunk_start = row.astype(F32) * float(STEPS)
+    pl.semaphore_wait(barrier, len(near) + 3)
+
+    def tell(k, partners):
+        for who in partners:
+            pl.semaphore_signal(st.at[k], inc=1, device_id=(who, y), device_id_type=MESH)
+
+    def halo_copy():
+        return pltpu.make_async_remote_copy(
+            src_ref=hal_s, dst_ref=hal_r, send_sem=h_s, recv_sem=h_r,
+            device_id=(nxt, y), device_id_type=MESH)
+
+    def rows_of(slot, part, parts):
+        size = 32 // parts
+        return wbuf.at[slot, pl.ds(part * size, size)]
+
+    def push(slot, part, parts, who, sem):
+        block = rows_of(slot, part, parts)
+        pltpu.make_async_remote_copy(
+            src_ref=block, dst_ref=block, send_sem=w_s, recv_sem=sem,
+            device_id=(who, y), device_id_type=MESH).start()
+
+    def landed(slot, part, parts, sem):
+        block = rows_of(slot, part, parts)
+        pltpu.make_async_copy(block, block, sem).wait()
+
+    def spread(slot, offset, part):
+        n = offset % 16
+        push(slot, part, OWN, xr, xf_r.at[0, n, part])
+        push(slot, part, OWN, xl, xf_r.at[1, n, part])
+
+    def slot_of(offset, xx):
+        return ((z + offset + 16) % 16) * 4 + (xx % 4)
+
+    ways = ((-1, zr), (1, zl))
+
+    def push_mine(part, parts, who, sem):
+        size = 32 // parts
+        pltpu.make_async_remote_copy(
+            src_ref=wt.at[pl.ds(part * size, size)], dst_ref=rows_of(me_slot, part, parts),
+            send_sem=w_s, recv_sem=sem, device_id=(who, y), device_id_type=MESH).start()
+
+    for part in range(OWN):
+        for way in range(2):
+            push_mine(part, OWN, ways[way][1], w_r.at[way, 0, part])
+    for part in range(OTHER):
+        push_mine(part, OTHER, xo, x2_r.at[part])
+    tell(0, (sib, xr, xl, xo, at(z + 2, x), at(z + 14, x)))
 
     fetches[0].wait()
     for b in range(3):
@@ -81,79 +125,35 @@
             hal_s[l, 2 * b : 2 * b + 2, :] = rows[14:16, l * 128 : (l + 1) * 128]
     for l in range(BLOCKS):
         hal_s[l, 6:8, :] = jnp.zeros((2, 128), F32)
-    row = lax.broadcasted_iota(jnp.int32, (8, 128), 0)
-    chunk_start = row.astype(F32) * float(STEPS)
-    fetches[1].wait()
-    pl.semaphore_wait(barrier, greetings)
-
-    def tell(k, far):
-        for step in (far, 16 - far):
-            pl.semaphore_signal(st.at[k], inc=1, device_id=(at(z + step, x), y), device_id_type=MESH)
-
-
-    def halo_copy():
-        return pltpu.make_async_remote_copy(
-            src_ref=hal_s, dst_ref=hal_r, send_sem=h_s, recv_sem=h_r,
-            device_id=(nxt, y), device_id_type=MESH)
-
     halo_copy().start()
-
-    def rows_of(slot, part, parts):
-        size = 32 // parts
-        return wbuf.at[slot, pl.ds(part * size, size)]
-
-    def push(slot, part, parts, who, sem):
-        block = rows_of(slot, part, parts)
-        pltpu.make_async_remote_copy(
-            src_ref=block, dst_ref=block, send_sem=w_s, recv_sem=sem,
-            device_id=(who, y), device_id_type=MESH).start()
-
-    def landed(slot, part, parts, sem):
-        block = rows_of(slot, part, parts)
-        pltpu.make_async_copy(block, block, sem).wait()
-
-    order = unit_offsets()
-
-    def spread(slot, offset, part):
-        n = order.index(offset)
-        push(slot, part, OWN, xr, xf_r.at[0, n, part])
-        push(slot, part, OWN, xl, xf_r.at[1, n, part])
-
-    def slot_of(offset, xx):
-        return ((z + offset + 16) % 16) * 4 + (xx % 4)
-
-    ways = ((-1, zr, 8), (1, zl, 7))
     for part in range(OWN):
-        for way in range(2):
-            push(me_slot, part, OWN, ways[way][1], w_r.at[way, 0, part])
-    for part in range(OTHER):
-        push(me_slot, part, OTHER, xo, x2_r.at[part])
-    for part in range(OWN):
-        spread(me_slot, 0, part)
-    tell(0, 2)
+        push_mine(part, OWN, xr, xf_r.at[0, 0, part])
+        push_mine(part, OWN, xl, xf_r.at[1, 0, part])
 
     def relay_own(k):
         for part in range(OWN):
-            for way, (sign, onward, last) in enumerate(ways):
+            for way, (sign, onward) in enumerate(ways):
+                last = 8 if part % 2 == way else 7
                 if k <= last:
                     slot = slot_of(sign * k, x)
                     landed(slot, part, OWN, w_r.at[way, k - 1, part])
                     if k < last:
                         push(slot, part, OWN, onward, w_r.at[way, k, part])
-            for sign, _, last in ways:
-                if k <= last:
+            for way, (sign, _) in enumerate(ways):
+                if k <= (8 if part % 2 == way else 7):
                     spread(slot_of(sign * k, x), sign * k, part)
 
     def relay_other(k):
         for part in range(OTHER):
-            for way, (sign, onward, last) in enumerate(ways):
+            for way, (sign, onward) in enumerate(ways):
+                last = 8 if part % 2 == way else 7
                 if k <= last:
                     slot = slot_of(sign * k, x + 2)
                     landed(slot, part, OTHER, w_r.at[2 + way, k - 1, part])
                     if k < last:
                         push(slot, part, OTHER, onward, w_r.at[2 + way, k, part])
 
-    for copy in fetches[2:]:
+    for copy in fetches[1:]:
         copy.wait()
     for l in range(BLOCKS):
         lanes = slice(l * 128, (l + 1) * 128)
@@ -237,8 +237,8 @@
 
     lax.fori_loop(0, 4, states, 0)
     relay_own(1)
-    pl.semaphore_wait(st.at[0], 2)
-    tell(1, 4)
+    pl.semaphore_wait(st.at[0], 6)
+    tell(1, (at(z + 4, x), at(z + 12, x)))
     lax.fori_loop(4, 8, states, 0)
 
     def member(d):
@@ -251,11 +251,9 @@
 
     ab[g] = sb[g]
 
-    def send_a(d, carry):
+    members = (4, 12, 5, 11, 3, 13, 8, 7, 9, 6, 10, 2, 14, 15, 1)
+    for d in members:
         to_member(sb.at[member(d)], ab.at[g], d, 0)
-        return carry
-
-    lax.fori_loop(1, 16, send_a, 0)
 
     def local(l, carry):
         us = [u_t[l, j] for j in range(STEPS)]
@@ -285,14 +283,11 @@
         total = total * hop + ab[h]
     tb[...] = total
 
-    def send_b(d, carry):
+    pl.semaphore_wait(st.at[1], 2)
+    for d in (4, 3, 5, 2, 6, 1, 7):
         pltpu.make_async_remote_copy(
             src_ref=tb, dst_ref=bb.at[d - 1], send_sem=ph_s.at[1], recv_sem=ph_r.at[1],
             device_id=(((grp + d) % 8) * 16 + g, y), device_id_type=MESH).start()
-        return carry
-
-    pl.semaphore_wait(st.at[1], 2)
-    lax.fori_loop(1, 8, send_b, 0)
     relay_own(3)
     relay_other(3)
     relay_own(4)
@@ -307,11 +302,8 @@
         state = state * hop + ab[h]
     cr[g] = cs[g]
 
-    def send_c(d, carry):
+    for d in members:
         to_member(cs.at[member(d)], cr.at[g], d, 2)
-        return carry
-
-    lax.fori_loop(1, 16, send_c, 0)
     relay_own(5)
     relay_other(5)
     group_wait(cr, 15, 2)
@@ -345,62 +337,74 @@
         gated(half).start()
         if half == 0:
             relay_own(6)
+
+    def distance(turn):
+        a, b, c_, d = (row[turn] % 16 for row in TURNS)
+        r = z % 4
+        return jnp.where(r == 0, a, jnp.where(r == 1, b, jnp.where(r == 2, c_, d)))
+
+    def units(*turns, cores=(0, 1)):
+        weights = []
+        for turn in turns:
+            n = distance(turn)
+            zq = (z + n) % 16
+            if 0 in cores:
+                for part in range(OWN):
+                    landed(zq * 4 + (x + 3) % 4, part, OWN, xf_r.at[0, n, part])
+                    landed(zq * 4 + (x + 1) % 4, part, OWN, xf_r.at[1, n, part])
+            weights.append(wbuf[pl.ds(zq * 4, 4)].reshape(128, 1024))
+        tokens = gb[cores[0] : cores[-1] + 1].reshape(128 * len(cores), 1024)
+        part = lax.dot_general(
+            tokens, jnp.concatenate(weights, axis=0), (((1,), (1,)), ((), ())),
+            preferred_element_type=F32).astype(BF16)
+        for i, turn in enumerate(turns):
+            for k, core in enumerate(cores):
+                ps[2 * turn + core] = part[k * 128 : (k + 1) * 128, i * 128 : (i + 1) * 128]
+                ship(turn, (z + distance(turn)) % 16, core)
+
+    def ship(n, zq, core):
+        owner, place = zq // 4, zq % 4
+        dy = (owner - y + 4) % 4
+
+        def copy(who):
+            pltpu.make_async_remote_copy(
+                src_ref=ps.at[2 * n + core], dst_ref=rb.at[dy, core, place], send_sem=rs_s,
+                recv_sem=rs_r.at[dy, core, place], device_id=(who, owner), device_id_type=MESH).start()
+
+        if core == 1:
+            copy(sib)
+        else:
+            @pl.when(dy != 0)
+            def _():
+                copy(ctx)
+
+            @pl.when(dy == 0)
+            def _():
+                rb[0, 0, place] = ps[2 * n]
+
+    units(0, 1, cores=(0,))
+    units(2, 3, cores=(0,))
     for half in range(2):
         gated(half).wait()
+    units(0, 1, cores=(1,))
+    units(2, 3, cores=(1,))
     relay_other(6)
-
-    def units(*offsets):
-        weights = []
-        for offset in offsets:
-            n = order.index(offset)
-            zq = (z + offset + 16) % 16
-            for part in range(OWN):
-                landed(zq * 4 + (x + 3) % 4, part, OWN, xf_r.at[0, n, part])
-                landed(zq * 4 + (x + 1) % 4, part, OWN, xf_r.at[1, n, part])
-            weights.append(wbuf[pl.ds(zq * 4, 4)].reshape(128, 1024))
-        part = lax.dot_general(
-            gb[...].reshape(256, 1024), jnp.concatenate(weights, axis=0), (((1,), (1,)), ((), ())),
-            preferred_element_type=F32).astype(BF16)
-        for i, offset in enumerate(offsets):
-            n = order.index(offset)
-            zq = (z + offset + 16) % 16
-            ps[2 * n] = part[:128, i * 128 : (i + 1) * 128]
-            ps[2 * n + 1] = part[128:, i * 128 : (i + 1) * 128]
-            ship(n, zq)
-
-    def ship(n, zq):
-        owner, place = zq // 4, zq % 4
-        dy = (owner - y + 4) % 4
-        pltpu.make_async_remote_copy(
-            src_ref=ps.at[2 * n + 1], dst_ref=rb.at[dy, 1, place], send_sem=rs_s,
-            recv_sem=rs_r.at[dy, 1, place], device_id=(sib, owner), device_id_type=MESH).start()
-
-        @pl.when(dy != 0)
-        def _():
-            pltpu.make_async_remote_copy(
-                src_ref=ps.at[2 * n], dst_ref=rb.at[dy, 0, place], send_sem=rs_s,
-                recv_sem=rs_r.at[dy, 0, place], device_id=(ctx, owner), device_id_type=MESH).start()
-
-        @pl.when(dy == 0)
-        def _():
-            rb[0, 0, place] = ps[2 * n]
-
-    units(0, 4)
-    units(-4, 1)
-    units(5, -3)
+    units(4, 5)
     relay_own(7)
-    units(-1, 3)
-    units(-5, 2)
+    units(6, 7)
     relay_other(7)
-    units(6, -2)
+    units(8, 9)
     relay_own(8)
-    units(-6, 7)
+    units(10, 11)
+    units(12, 13)
+    units(14)
     relay_other(8)
-    units(-7)
-    units(-8)
+    units(15)
 
     lane = lax.broadcasted_iota(jnp.int32, (128, 128), 1) // 32
-    for place in range(4):
+    first = (4 * y - z + 16) % 16
+    for turn in range(4):
+        place = jnp.where(first < 8, turn, 3 - turn)
         sums = []
         for core in range(2):
             rel = (core + c) % 2
@@ -421,8 +425,9 @@
 
         a32, a64, a96 = (pltpu.roll(a, s, 1) for s in (32, 64, 96))
         b32, b64, b96 = (pltpu.roll(b, s, 1) for s in (32, 64, 96))
-        out[:, place * 256 : place * 256 + 128] = pick((a, b32, a32, b64)).astype(BF16)
-        out[:, place * 256 + 128 : place * 256 + 256] = pick((a64, b96, a96, b)).astype(BF16)
+        at0 = pl.multiple_of(place * 256, 128)
+        out[:, pl.ds(at0, 128)] = pick((a, b32, a32, b64)).astype(BF16)
+        out[:, pl.ds(pl.multiple_of(at0 + 128, 128), 128)] = pick((a64, b96, a96, b)).astype(BF16)
 
     part = wbuf.at[pl.ds(0, 63)]
     pltpu.make_async_copy(part, part, w_s).wait()

time: 62.2 us -> 59.2 us (0.952)
  the two profiles are of different devices: /device:TPU:48 before, /device:TPU:1 now
where the time goes in v3:
time: 59.2 us; the launch traced here: 59 us
  Pallas kernels  57.3 us (97%)
  local copies, waits for them, and re-layouts  1.67 us (3%)
    pallas_call x1, Pallas kernels, on_device(): pl.pallas_call(kernel, out_shape=jax.ShapeDtypeStruct((128, 1024), BF16),...  57.3 us
    unnamed x1, local copies, waits for them, and re-layouts  1.67 us

profile of v3, /device:TPU:1, one launch (start us, length us, event | category | flops | bytes accessed | tf_op | source)
XLA Modules:
  0.0 59.0 jit_solution(2564006058757389525)
XLA Ops:
  0.0 57.3 %hyena.1 = bf16[128,1024]{1,0:T(8,128)(2,1)} custom-call(bf16[3,128,1024]{2,1,0:T(8,128)(2,1)} %proj_h.1, f32[3,3,1024]{2,1,0:T(4,128)} %sfilt_h.1, f32[16,1024]{1,0:T(8,128)} %bitcast.4, f32[16,1024]{1,0:T(8,128)} %bitcast.5, f32[1,1024]{1,0:T(1,128)} %bitcast.7, bf16[32,1024]{1,0:T(8,128)(2,1)} %bitcast.6), custom_call_target="tpu_custom_call" | custom-call | flops 2147483648 | bytes 2097152 | tf_op jit(solution)/shard_map/hyena/pallas_call | solution.py:445
  57.4 1.7 %copy.8 = bf16[128,1024]{1,0:T(8,128)(2,1)} copy(bf16[128,1024]{1,0:T(8,128)(2,1)} %hyena.1) | data formatting | bytes 524288

commit v4 on v3

--- a/solution.py
+++ b/solution.py
@@ -126,9 +126,6 @@
     for l in range(BLOCKS):
         hal_s[l, 6:8, :] = jnp.zeros((2, 128), F32)
     halo_copy().start()
-    for part in range(OWN):
-        push_mine(part, OWN, xr, xf_r.at[0, 0, part])
-        push_mine(part, OWN, xl, xf_r.at[1, 0, part])
 
     def relay_own(k):
         for part in range(OWN):
@@ -288,6 +285,9 @@
         pltpu.make_async_remote_copy(
             src_ref=tb, dst_ref=bb.at[d - 1], send_sem=ph_s.at[1], recv_sem=ph_r.at[1],
             device_id=(((grp + d) % 8) * 16 + g, y), device_id_type=MESH).start()
+    for part in range(OWN):
+        push_mine(part, OWN, xr, xf_r.at[0, 0, part])
+        push_mine(part, OWN, xl, xf_r.at[1, 0, part])
     relay_own(3)
     relay_other(3)
     relay_own(4)

time: 59.2 us -> 58.7 us (level)
  no operation moved by 1% of the time
where the time goes in v4:
time: 58.7 us; the launch traced here: 58.5 us
  Pallas kernels  56.9 us (97%)
  local copies, waits for them, and re-layouts  1.67 us (3%)
    pallas_call x1, Pallas kernels, on_device(): pl.pallas_call(kernel, out_shape=jax.ShapeDtypeStruct((128, 1024), BF16),...  56.9 us
    unnamed x1, local copies, waits for them, and re-layouts  1.67 us

profile of v4, /device:TPU:1, one launch (start us, length us, event | category | flops | bytes accessed | tf_op | source)
XLA Modules:
  0.0 58.5 jit_solution(13709033567840764705)
XLA Ops:
  0.0 56.9 %hyena.1 = bf16[128,1024]{1,0:T(8,128)(2,1)} custom-call(bf16[3,128,1024]{2,1,0:T(8,128)(2,1)} %proj_h.1, f32[3,3,1024]{2,1,0:T(4,128)} %sfilt_h.1, f32[16,1024]{1,0:T(8,128)} %bitcast.4, f32[16,1024]{1,0:T(8,128)} %bitcast.5, f32[1,1024]{1,0:T(1,128)} %bitcast.7, bf16[32,1024]{1,0:T(8,128)(2,1)} %bitcast.6), custom_call_target="tpu_custom_call" | custom-call | flops 2147483648 | bytes 2097152 | tf_op jit(solution)/shard_map/hyena/pallas_call | solution.py:445
  56.9 1.7 %copy.8 = bf16[128,1024]{1,0:T(8,128)(2,1)} copy(bf16[128,1024]{1,0:T(8,128)(2,1)} %hyena.1) | data formatting | bytes 524288

commit v5 on v4

--- a/solution.py
+++ b/solution.py
@@ -28,7 +28,7 @@
 def kernel(
     proj_h, sfilt_h, res_h, dec_h, skip_h, wt, out,
     proj, sfilt, res, dec, skip,
-    x32, lam_t, al_t, l16_t, l32_t, l64_t, taps_t, sf_t, l128_t, l2048_t, pow_t, z_t, q_t, u_t, y_t, gt,
+    x32, lam_t, al_t, l16_t, l32_t, l64_t, l127_t, l126_t, cor_t, kv_t, taps_t, sf_t, l128_t, l2048_t, pow_t, z_t, q_t, u_t, y_t, gt,
     hal_s, hal_r, sb, ab, tb, bb, cs, cr, wbuf, gb, ps, rb,
     in_s, h_s, h_r, w_s, w_r, x2_r, xf_r, ph_s, ph_r, g_s, g_r, rs_s, rs_r, st,
 ):
@@ -161,6 +161,8 @@
         l16_t[l] = jnp.exp(-16.0 * rate)
         l32_t[l] = jnp.exp(-32.0 * rate)
         l64_t[l] = jnp.exp(-64.0 * rate)
+        l127_t[l] = jnp.exp(-127.0 * rate)
+        l126_t[l] = jnp.exp(-126.0 * rate)
         hop = jnp.exp(-128.0 * rate)
         far = jnp.exp(-2048.0 * rate)
         for half in range(2):
@@ -192,26 +194,18 @@
     def res_block(l):
         return res[:, pl.ds(pl.multiple_of(l * 128, 128), 128)]
 
-    other = slot_of(0, x + 2)
-    for part in range(OTHER):
-        landed(other, part, OTHER, x2_r.at[part])
-        push(other, part, OTHER, zr, w_r.at[2, 0, part])
-        push(other, part, OTHER, zl, w_r.at[3, 0, part])
-
-    halo_copy().wait()
     known = jnp.where(ctx == 0, 0.0, 1.0).astype(F32)
     keep1 = jnp.where(row >= 1, 1.0, 0.0).astype(F32)
     keep2 = jnp.where(row >= 2, 1.0, 0.0).astype(F32)
     keep4 = jnp.where(row >= 4, 1.0, 0.0).astype(F32)
 
     def states(l, carry):
-        halo = hal_r[l] * known
         filt = sf_t[l]
         shorts = []
         for b in range(3):
             xs = [x32[b, l, pl.ds(j, 8, stride=STEPS), :] for j in range(STEPS)]
-            before1 = jnp.where(row >= 1, pltpu.roll(xs[15], 1, 0), halo[2 * b + 1 : 2 * b + 2, :])
-            before2 = jnp.where(row >= 1, pltpu.roll(xs[14], 1, 0), halo[2 * b : 2 * b + 1, :])
+            before1 = pltpu.roll(xs[15], 1, 0) * keep1
+            before2 = pltpu.roll(xs[14], 1, 0) * keep1
             line = [before2, before1] + xs
             f0, f1, f2 = (filt[3 * b + i : 3 * b + i + 1, :] for i in range(3))
             shorts.append([f0 * line[j + 2] + f1 * line[j + 1] + f2 * line[j] for j in range(STEPS)])
@@ -219,6 +213,8 @@
         for j in range(STEPS):
             q_t[l, j] = shorts[0][j]
             u_t[l, j] = us[j]
+        for j in range(2):
+            kv_t[l, j], kv_t[l, 2 + j] = shorts[1][j], shorts[2][j]
         lam, l16, l32, l64 = lam_t[l], l16_t[l], l32_t[l], l64_t[l]
         for m in range(MODES):
             rate = jnp.broadcast_to(lam[m : m + 1, :], (8, 128))
@@ -232,11 +228,41 @@
             sb[(m // 8) * 8 + l, m % 8 : m % 8 + 1, :] = end[7:8, :]
         return carry
 
+    first_row = jnp.where(row == 0, 1.0, 0.0).astype(F32) * known
+
+    def join(l, carry):
+        halo = hal_r[l]
+        filt = sf_t[l]
+        adds = []
+        for b in range(3):
+            old2, old1 = halo[2 * b : 2 * b + 1, :], halo[2 * b + 1 : 2 * b + 2, :]
+            f1, f2 = (filt[3 * b + i : 3 * b + i + 1, :] for i in (1, 2))
+            adds.append((first_row * (f1 * old1 + f2 * old2), first_row * (f2 * old1)))
+        deltas = []
+        for j in range(2):
+            q_t[l, j] = q_t[l, j] + adds[0][j]
+            u = ((kv_t[l, j] + adds[1][j]) * (kv_t[l, 2 + j] + adds[2][j])).astype(BF16).astype(F32)
+            deltas.append((u - u_t[l, j])[0:1, :])
+            u_t[l, j] = u
+        end = l127_t[l] * deltas[0] + l126_t[l] * deltas[1]
+        sb[l] = sb[l] + end[:8]
+        sb[8 + l] = sb[8 + l] + end[8:]
+        grow = jnp.exp(dec_block(l))
+        cor_t[l] = grow * (deltas[0] + grow * deltas[1])
+        return carry
+
     lax.fori_loop(0, 4, states, 0)
+    other = slot_of(0, x + 2)
+    for part in range(OTHER):
+        landed(other, part, OTHER, x2_r.at[part])
+        push(other, part, OTHER, zr, w_r.at[2, 0, part])
+        push(other, part, OTHER, zl, w_r.at[3, 0, part])
+    lax.fori_loop(4, 8, states, 0)
     relay_own(1)
+    halo_copy().wait()
+    lax.fori_loop(0, BLOCKS, join, 0)
     pl.semaphore_wait(st.at[0], 6)
     tell(1, (at(z + 4, x), at(z + 12, x)))
-    lax.fori_loop(4, 8, states, 0)
 
     def member(d):
         return (g + d) % 16
@@ -310,11 +336,11 @@
 
     def finish(l, carry):
         ys = [y_t[l, j] for j in range(STEPS)]
-        lam, al = lam_t[l], al_t[l]
+        lam, al, cor = lam_t[l], al_t[l], cor_t[l]
         tiles = [cr[l], cr[8 + l]]
         for m in range(MODES):
             rate = jnp.broadcast_to(lam[m : m + 1, :], (8, 128))
-            start = z_t[l, m] + pow_t[l, m] * tiles[m // 8][m % 8 : m % 8 + 1, :]
+            start = z_t[l, m] + pow_t[l, m] * (tiles[m // 8][m % 8 : m % 8 + 1, :] + keep1 * cor[m : m + 1, :])
             term = start * al[m : m + 1, :]
             for j in range(STEPS):
                 ys[j] = ys[j] + term
@@ -451,7 +477,7 @@
             vm((3, 128, 1024), BF16), vm((3, 3, 1024), F32), vm((16, 1024), F32), vm((16, 1024), F32), vm((1, 1024), F32),
             vm((3, 8, 128, 128), F32),
             vm(tile, F32), vm(tile, F32), vm(tile, F32), vm(tile, F32), vm(tile, F32),
-            vm(tile, F32), vm(tile, F32),
+            vm(tile, F32), vm(tile, F32), vm(tile, F32), vm((8, 4, 8, 128), F32), vm(tile, F32), vm(tile, F32),
             vm((16, 8, 128), F32), vm((16, 8, 128), F32),
             vm((8, 16, 8, 128), F32), vm((8, 16, 8, 128), F32),
             vm((8, 16, 8, 128), F32), vm((8, 16, 8, 128), F32), vm((8, 16, 8, 128), F32),

time: 58.7 us -> 59.1 us (level)
  no operation moved by 1% of the time
where the time goes in v5:
time: 59.1 us; the launch traced here: 58.9 us
  Pallas kernels  57.3 us (97%)
  local copies, waits for them, and re-layouts  1.67 us (3%)
    pallas_call x1, Pallas kernels, on_device(): pl.pallas_call(kernel, out_shape=jax.ShapeDtypeStruct((128, 1024), BF16),...  57.3 us
    unnamed x1, local copies, waits for them, and re-layouts  1.67 us

profile of v5, /device:TPU:1, one launch (start us, length us, event | category | flops | bytes accessed | tf_op | source)
XLA Modules:
  0.0 58.9 jit_solution(2783897587480170645)
XLA Ops:
  0.0 57.3 %hyena.1 = bf16[128,1024]{1,0:T(8,128)(2,1)} custom-call(bf16[3,128,1024]{2,1,0:T(8,128)(2,1)} %proj_h.1, f32[3,3,1024]{2,1,0:T(4,128)} %sfilt_h.1, f32[16,1024]{1,0:T(8,128)} %bitcast.4, f32[16,1024]{1,0:T(8,128)} %bitcast.5, f32[1,1024]{1,0:T(1,128)} %bitcast.7, bf16[32,1024]{1,0:T(8,128)(2,1)} %bitcast.6), custom_call_target="tpu_custom_call" | custom-call | flops 2147483648 | bytes 2097152 | tf_op jit(solution)/shard_map/hyena/pallas_call | solution.py:471
  57.3 1.7 %copy.8 = bf16[128,1024]{1,0:T(8,128)(2,1)} copy(bf16[128,1024]{1,0:T(8,128)(2,1)} %hyena.1) | data formatting | bytes 524288
